TPU v7x, 32 devices: a whole 2x2x4 slice. The times are simulated.
32 devices in a mesh: sec: 2 (over y), exp: 8 (over z, x), hid: 2 (over core).
Axes of the slice: x: 2, y: 2, z: 4, core: 2. Of those that a mesh axis runs over, the one named last changes fastest.
Arguments:
- tokens: bfloat16 [1024, 4096], P('exp', ('sec', 'hid')), may hold values from -1200 to 1200
- norm_gain: bfloat16 [4096], P(('sec', 'hid')), may hold values from 0.5 to 2
- route_weight: float32 [1024, 2], P('exp'), may hold values from 0.1 to 1
- block_experts: int32 [8, 2], replicated, may hold values from 0 to 7, all different within a row; in each aligned block of 8 rows (0 to 7, 8 to 15, ...) at most 4 rows name the same one
- w_gate: bfloat16 [2, 4096, 32768], P('sec', None, ('exp', 'hid')), may hold values from -0.09375 to 0.09375
- w_up: bfloat16 [2, 4096, 32768], P('sec', None, ('exp', 'hid')), may hold values from -0.09375 to 0.09375
- w_down: bfloat16 [2, 32768, 4096], P('sec', ('exp', 'hid')), may hold values from -0.0625 to 0.0625
Outputs:
- moe_out: bfloat16 [1024, 4096], P('exp', ('sec', 'hid'))
Inputs may be any that keep to these rules, and one draw needn't show every extreme that they name: `block_experts`: each row names 2 different experts; no expert is named by more than 4 rows, a bound that some block reaches; every expert is named by some row.
All inputs are finite; a program needn't handle non-finite values.
Results may differ from a plain program's by a relative error of at most 0.018.
Values may be sent and summed in bfloat16 or wider, within the bound.
A program may use at most 128 MiB of HBM per device.

v0:
```python
import jax
import jax.numpy as jnp
from jax import lax
from jax.sharding import PartitionSpec as P

EXPERTS = 8
BLK = 128
MOST = 4


def per_device(tokens, norm_gain, route_weight, block_experts, w_gate, w_up, w_down):
    exp_devices = lax.axis_size("exp")
    group_size = exp_devices // EXPERTS
    my_expert = lax.axis_index("exp") // group_size
    tok_local = tokens.shape[0]
    total_rows = tok_local * exp_devices
    num_blocks = total_rows // BLK
    slot_count = MOST
    gate_local = w_gate[0]
    up_local = w_up[0]
    down_local = w_down[0]
    block_hit = jnp.any(block_experts == my_expert, axis=1)
    hit_flags = block_hit.astype(jnp.int32)
    slot_of_block = jnp.where(block_hit, jnp.cumsum(hit_flags) - 1, -1)
    slot_ids = jnp.arange(slot_count, dtype=jnp.int32)
    slot_match = slot_of_block[None, :] == slot_ids[:, None]
    block_ids = jnp.arange(num_blocks, dtype=jnp.int32)
    block_of_slot = jnp.sum(jnp.where(slot_match, block_ids[None, :], 0), axis=1)
    slot_valid = jnp.any(slot_match, axis=1)
    gathered = lax.all_gather(tokens, "exp", axis=0, tiled=True)
    width = gathered.shape[1]
    picked = jnp.take(gathered.reshape(num_blocks, BLK, width), block_of_slot, axis=0)
    picked = jnp.where(slot_valid[:, None, None], picked, jnp.zeros_like(picked))
    picked_rows = picked.reshape(slot_count * BLK, width)
    full_rows, full_gain = (
        lax.all_gather(picked_rows, ("sec", "hid"), axis=1, tiled=True),
        lax.all_gather(norm_gain, ("sec", "hid"), axis=0, tiled=True),
    )
    values = full_rows.astype(jnp.float32)
    rms_value = jnp.sqrt(jnp.mean(values * values, axis=1, keepdims=True) + 1e-05)
    normed = (values * full_gain.astype(jnp.float32) / rms_value).astype(jnp.bfloat16)
    gate_acc = jnp.dot(normed, gate_local, preferred_element_type=jnp.float32)
    up_acc = jnp.dot(normed, up_local, preferred_element_type=jnp.float32)
    activated = (jax.nn.silu(gate_acc) * up_acc).astype(jnp.bfloat16)
    contribution = jnp.dot(activated, down_local, preferred_element_type=jnp.float32)
    term_vals = contribution.astype(jnp.bfloat16)
    own_rows = lax.axis_index("exp") * tok_local + jnp.arange(tok_local, dtype=jnp.int32)
    own_blocks = own_rows // BLK
    own_experts = jnp.take(block_experts, own_blocks, axis=0)
    source_expert = jnp.arange(exp_devices, dtype=jnp.int32) // group_size
    factor = jnp.sum(
        jnp.where(
            own_experts[None, :, :] == source_expert[:, None, None], route_weight[None, :, :], 0.0
        ),
        axis=2,
    )
    reduced = lax.psum_scatter(term_vals, ("sec", "hid"), scatter_dimension=1, tiled=True).astype(
        jnp.float32
    )
    width = reduced.shape[1]
    slot_grid = reduced.reshape(slot_count, BLK, width)
    safe_slot = jnp.maximum(slot_of_block, 0)
    expanded = jnp.take(slot_grid, safe_slot, axis=0)
    expanded = jnp.where(block_hit[:, None, None], expanded, jnp.zeros_like(expanded))
    outgoing = expanded.reshape(exp_devices, tok_local, width)
    received = lax.all_to_all(
        outgoing.astype(jnp.bfloat16), "exp", split_axis=0, concat_axis=0, tiled=True
    ).astype(outgoing.dtype)
    result = jnp.sum(received * factor[:, :, None], axis=0)
    return result.astype(jnp.bfloat16)


def solution(mesh):
    return jax.shard_map(
        per_device,
        mesh=mesh,
        in_specs=(
            P("exp", ("sec", "hid")),
            P(("sec", "hid")),
            P("exp", None),
            P(),
            P("sec", None, ("exp", "hid")),
            P("sec", None, ("exp", "hid")),
            P("sec", ("exp", "hid"), None),
        ),
        out_specs=P("exp", ("sec", "hid")),
        check_vma=False,
    )
```

profile of v0, /device:TPU:0, one launch (start us, length us, event | category | flops | bytes accessed | tf_op | source)
XLA Modules:
  0.0 257.4 jit_solution(6095783637274674811)
XLA Ops:
  6.5 0.0 all-gather.3.cloned.1.call-start
  6.5 0.7 all-gather.3.cloned.1.call-update
  7.3 0.0 all-gather.5.cloned.1.call-start
  7.3 0.7 compare_reduce_fusion
  8.0 0.2 reduce-window.4
  8.2 0.1 fusion.18
  8.3 0.1 select_reduce_fusion.1
  8.5 0.1 broadcast_bitcast_fusion
  8.6 53.0 %all-gather.3.cloned.1.call-done = bf16[1024,1024]{1,0:T(8,128)(2,1)} async-done(((bf16[128,1024]{1,0:T(8,128)(2,1)}), bf16[1024,1024]{1,0:T(8,128)(2,1)}) %all-gather.3.cloned.1.call-update) | async-done | bytes 2097168 | tf_op jit(solution)/shard_map/all_gather | solution.py:30
  61.5 2.2 gather_fusion
  63.7 1.2 fusion.17
  64.9 0.0 all-gather.5.cloned.1.call-update
  65.0 0.0 reduce-scatter.2.cloned.1.call-start
  65.0 5.2 %all_gather.11 = bf16[4096]{0:T(1024)(128)(2,1)S(1)} all-gather(bf16[1024]{0:T(1024)(128)(2,1)S(1)} %copy-done.2), channel_id=1, replica_groups=mesh['sec'=2,'exp'=8,'hid'=2] {'sec','hid'}, dimensions={0}, use_global_device_ids=true | all-gather | bytes 10240 | tf_op jit(solution)/shard_map/all_gather | solution.py:37
  70.2 27.9 %all-gather.5.cloned.1.call-done = bf16[512,4096]{1,0:T(8,128)(2,1)} async-done(((bf16[512,1024]{1,0:T(8,128)(2,1)}), bf16[512,4096]{1,0:T(8,128)(2,1)}) %all-gather.5.cloned.1.call-update) | async-done | bytes 4194320 | tf_op jit(solution)/shard_map/all_gather | solution.py:36
  98.1 3.2 %fusion.8 = f32[512]{0:T(512)S(1)} fusion(bf16[512,4096]{1,0:T(8,128)(2,1)} %all-gather.5.cloned.1.call-done), kind=kLoop, calls=%fused_computation.13 | loop fusion | flops 6290944 | bytes 4196352 | tf_op jit(solution)/shard_map/reduce_sum | solution.py:40
  101.3 0.2 copy-done
  101.6 14.0 %fusion.4 = f32[512,2048]{1,0:T(8,128)} fusion(bf16[1,4096,2048]{2,1,0:T(8,128)(2,1)} %param.11, bf16[512,4096]{1,0:T(8,128)(2,1)S(1)} %copy-done, f32[512]{0:T(512)S(1)} %add_sqrt_fusion, f32[4096]{0:T(1024)S(1)} %convert_element_type.37), kind=kOutput, calls=%fused_computation.7 | convolution fusion | flops 8598323200 | bytes 25184256 | tf_op jit(solution)/shard_map/dot_general | solution.py:42
  115.5 31.7 %fusion.9 = bf16[512,4096]{1,0:T(8,128)(2,1)} fusion(bf16[1,2048,4096]{2,1,0:T(8,128)(2,1)} %param.13, f32[512,2048]{1,0:T(8,128)} %fusion.4, bf16[1,4096,2048]{2,1,0:T(8,128)(2,1)} %param.12, bf16[512,4096]{1,0:T(8,128)(2,1)} %all-gather.5.cloned.1.call-done, f32[512]{0:T(512)S(1)} %add_sqrt_fusion, f32[4096]{0:T(1024)S(1)} %convert_element_type.37), kind=kOutput, calls=%fused_computation.14 | convolution fusion | flops 17196646400 | bytes 46155776 | tf_op jit(solution)/shard_map/dot_general | solution.py:45
  147.3 0.0 reduce-scatter.2.cloned.1.call-update
  147.3 44.7 %reduce-scatter.2.cloned.1.call-done = bf16[512,1024]{1,0:T(8,128)(2,1)} async-done(((bf16[512,4096]{1,0:T(8,128)(2,1)}), bf16[512,1024]{1,0:T(8,128)(2,1)}) %reduce-scatter.2.cloned.1.call-update) | async-done | bytes 1048592 | tf_op jit(solution)/shard_map/reduce_scatter | solution.py:57
  192.0 1.9 gather_fusion.1
  193.9 0.0 copy-start.1
  193.9 0.0 copy-start.3
  193.9 2.0 select_convert_fusion
  195.9 5.5 %all-to-all-start = ((bf16[8,128,1024]{2,1,0:T(8,128)(2,1)}), bf16[8,128,1024]{2,1,0:T(8,128)(2,1)S(1)}, u32[]{:S(2)}, u32[]{:S(2)}) async-start(bf16[8,128,1024]{2,1,0:T(8,128)(2,1)} %select_convert_fusion), calls=%async_computation.1 | async-start | bytes 4194304 | tf_op jit(solution)/shard_map/all_to_all | solution.py:66
  201.4 0.1 copy.12
  201.5 0.6 gather_fusion.2
  202.2 0.1 broadcast_select_fusion
  202.3 0.1 copy.13
  202.4 47.3 %all-to-all-done = bf16[8,128,1024]{2,1,0:T(8,128)(2,1)S(1)} async-done(((bf16[8,128,1024]{2,1,0:T(8,128)(2,1)}), bf16[8,128,1024]{2,1,0:T(8,128)(2,1)S(1)}, u32[]{:S(2)}, u32[]{:S(2)}) %all-to-all-start) | async-done | bytes 2097184 | tf_op jit(solution)/shard_map/all_to_all | solution.py:66
  249.7 1.2 multiply_reduce_fusion
  (18 shorter events, 0.1 us)
Async XLA Ops:
  6.5 58.5 %copy-start.2 = (bf16[1024]{0:T(1024)(128)(2,1)S(1)}, bf16[1024]{0:T(1024)(128)(2,1)}, u32[]{:S(2)}) copy-start(bf16[1024]{0:T(1024)(128)(2,1)} %param.8) | copy-start | bytes 6148
  6.5 55.0 %all-gather.3.cloned.1.call-start = ((), (), s32[]{:S(2)}) async-start(), calls=%async_computation.2 | async-start | bytes 2359296 | tf_op jit(solution)/shard_map/all_gather | solution.py:30
  7.3 90.8 %all-gather.5.cloned.1.call-start = ((), (), s32[]{:S(2)}) async-start(), calls=%async_computation.3 | async-start | bytes 5242880 | tf_op jit(solution)/shard_map/all_gather | solution.py:36
  65.0 127.0 %reduce-scatter.2.cloned.1.call-start = ((), (), s32[]{:S(2)}) async-start(), calls=%async_computation.4 | async-start | bytes 5242880 | tf_op jit(solution)/shard_map/reduce_scatter | solution.py:57
  98.1 3.4 %copy-start = (bf16[512,4096]{1,0:T(8,128)(2,1)S(1)}, bf16[512,4096]{1,0:T(8,128)(2,1)}, u32[]{:S(2)}) copy-start(bf16[512,4096]{1,0:T(8,128)(2,1)} %all-gather.5.cloned.1.call-done) | copy-start | bytes 12582916
  193.9 7.5 %copy-start.1 = (s32[8,2]{0,1:T(2,128)S(1)}, s32[8,2]{0,1:T(2,128)}, u32[]{:S(2)}) copy-start(s32[8,2]{0,1:T(2,128)} %param.10) | copy-start | bytes 196
  193.9 8.5 %copy-start.3 = (f32[128,2]{0,1:T(2,128)S(1)}, f32[128,2]{0,1:T(2,128)}, u32[]{:S(2)}) copy-start(f32[128,2]{0,1:T(2,128)} %param.9) | copy-start | bytes 3076
  195.9 53.8 %all-to-all-start = ((bf16[8,128,1024]{2,1,0:T(8,128)(2,1)}), bf16[8,128,1024]{2,1,0:T(8,128)(2,1)S(1)}, u32[]{:S(2)}, u32[]{:S(2)}) async-start(bf16[8,128,1024]{2,1,0:T(8,128)(2,1)} %select_convert_fusion), calls=%async_computation.1 | async-start | bytes 4194304 | tf_op jit(solution)/shard_map/all_to_all | solution.py:66
Sparse Core Ops, SparseCore 0:
  9.5 51.9 all-gather.2
  65.1 32.9 all-gather.4
  147.4 44.5 reduce-scatter.1
where the time goes:
time: 258 us; the launch traced here: 257 us
  waiting for transfers between devices  174 us (67%)
  matrix products  45.7 us (18%)
  between operations  13.2 us (5%)
  other arithmetic  8.95 us (3%)
  starting transfers between devices  5.6 us (2%)
  local copies, waits for them, and re-layouts  5.19 us (2%)
  blocking collectives  5.16 us (2%)
    all_gather x1, waiting for transfers between devices, per_device(): gathered = lax.all_gather(tokens, 'exp', axis=0, tiled=True)  53 us
    all_to_all x1, waiting for transfers between devices, per_device(): lax.all_to_all(outgoing.astype(jnp.bfloat16), 'exp', split_axis=0, concat...  47.3 us
    reduce_scatter x1, waiting for transfers between devices, per_device(): lax.psum_scatter(term_vals, ('sec', 'hid'), scatter_dimension=1, tiled=True)  44.7 us
    dot_general x1, matrix products, per_device(): jnp.dot(activated, down_local, preferred_element_type=jnp.float32)  31.7 us
    all_gather x1, waiting for transfers between devices, per_device(): lax.all_gather(picked_rows, ('sec', 'hid'), axis=1, tiled=True)  27.9 us
    dot_general x1, matrix products, per_device(): gate_acc = jnp.dot(normed, gate_local, preferred_element_type=jnp.float32)  14 us
    all_to_all x1, starting transfers between devices, per_device(): lax.all_to_all(outgoing.astype(jnp.bfloat16), 'exp', split_axis=0, concat...  5.52 us
    all_gather x1, blocking collectives, per_device(): lax.all_gather(norm_gain, ('sec', 'hid'), axis=0, tiled=True)  5.16 us
  transfers between devices with their start and end apart: 4, of which 4 were waited for; matrix products, arithmetic and copies ran while one was open for 1% of the time, Pallas kernels for 0%

commit v1 on v0

v1 whole, which is shorter than its diff:
```python
import functools

import jax
import jax.numpy as jnp
from jax import lax
from jax.experimental import pallas as pl
from jax.experimental.pallas import tpu as pltpu
from jax.sharding import PartitionSpec as P

EXPERTS = 8
BLK = 128
MOST = 4
MESH = pl.DeviceIdType.MESH
EXTRA = 16


def greet(n, hid):
    e, s, h = lax.axis_index("exp"), lax.axis_index("sec"), lax.axis_index("hid")
    i, par = e // 2, e % 2
    barrier = pltpu.get_barrier_semaphore()
    for k in range(1, n):
        peer = lax.rem(i + k, n) * 2 + par
        pl.semaphore_signal(barrier, inc=1, device_id={"exp": peer}, device_id_type=MESH)
    pl.semaphore_signal(barrier, inc=1, device_id={"exp": i * 2 + 1 - par}, device_id_type=MESH)
    pl.semaphore_signal(barrier, inc=1, device_id={"sec": 1 - s}, device_id_type=MESH)
    for k in range(1, hid):
        pl.semaphore_signal(barrier, inc=1, device_id={"hid": lax.rem(h + k, hid)}, device_id_type=MESH)
    pl.semaphore_wait(barrier, (n - 1) + 1 + 1 + (hid - 1))
    return e, i, par, s, h


def remote(src, dst, sems, where, device):
    return pltpu.make_async_remote_copy(
        src_ref=src, dst_ref=dst, send_sem=sems[0].at[where], recv_sem=sems[1].at[where],
        device_id=device, device_id_type=MESH,
    )


def gather_kernel(n, hid, tok_ref, gain_ref, bos_ref, out_ref, gathered, full,
                  zs, zr, xs, xr, ys, yr, hs, hr, gs, gr):
    e, i, par, s, h = greet(n, hid)
    tl, width = tok_ref.shape
    slots = MOST * BLK

    def rows_of(index):
        return gathered.at[index * tl // BLK, pl.ds(pl.multiple_of(lax.rem(index * tl, BLK), tl), tl), :]

    mine = rows_of(e)
    mine[...] = tok_ref[...]
    pair = {"exp": i * 2 + 1 - par}
    far = []
    for k in range(1, n):
        c = remote(mine, mine, (zs, zr), k, {"exp": lax.rem(i + k, n) * 2 + par})
        c.start()
        far.append(c)
    near = [remote(mine, mine, (xs, xr), 0, pair)]
    near[0].start()
    for k in range(1, n):
        far[k - 1].wait_recv()
        got = rows_of(lax.rem(i - k + n, n) * 2 + par)
        c = remote(got, got, (xs, xr), k, pair)
        c.start()
        near.append(c)
    for c in near:
        c.wait_recv()

    me = s * hid + h
    over = (1 - s) * hid + h
    full[me, slots:, :] = jnp.broadcast_to(gain_ref[...], (EXTRA, width))
    parts = [pl.ds(k * BLK, BLK) for k in range(MOST)]
    parts[-1] = pl.ds((MOST - 1) * BLK, BLK + EXTRA)
    side, own, passed = [], [], []
    for k in range(MOST):
        full[me, k * BLK:(k + 1) * BLK, :] = gathered[bos_ref[k]]
        ref = full.at[me, parts[k], :]
        c = remote(ref, ref, (ys, yr), k, {"sec": 1 - s})
        c.start()
        side.append(c)
        for q in range(1, hid):
            c = remote(ref, ref, (hs, hr), k * hid + q, {"hid": lax.rem(h + q, hid)})
            c.start()
            own.append(c)
    for k in range(MOST):
        side[k].wait_recv()
        ref = full.at[over, parts[k], :]
        for q in range(1, hid):
            c = remote(ref, ref, (gs, gr), k * hid + q, {"hid": lax.rem(h + q, hid)})
            c.start()
            passed.append(c)
    for c in own + passed:
        c.wait_recv()
    groups = 2 * hid

    def norm(step, carry):
        rows = pl.ds(pl.multiple_of(step * 32, 32), 32)
        total = jnp.zeros((32, 1), jnp.float32)
        for j in range(groups):
            v = full[j, rows, :].astype(jnp.float32)
            total = total + jnp.sum(v * v, axis=1, keepdims=True)
        rms = jnp.sqrt(total / (groups * width) + 1e-05)
        for j in range(groups):
            v = full[j, rows, :].astype(jnp.float32)
            gain = full[j, slots:slots + EXTRA, :].astype(jnp.float32)[0:1, :]
            out_ref[rows, j * width:(j + 1) * width] = (v * gain / rms).astype(out_ref.dtype)
        return carry

    lax.fori_loop(0, slots // 32, norm, 0)
    for c in far + near + side + own + passed:
        c.wait_send()


def reduce_kernel(n, hid, term_ref, fac_ref, slot_ref, out_ref, hbuf, ysend, ybuf, red, spread,
                  psend, pbuf, qsend, qbuf, hs, hr, ys, yr, xs, xr, zs, zr):
    e, i, par, s, h = greet(n, hid)
    tl, width = out_ref.shape

    def cols(sec, at):
        return pl.ds(pl.multiple_of((sec * hid + at) * width, width), width)

    first = []
    for k in range(MOST):
        rows = pl.ds(k * BLK, BLK)
        for side in range(2):
            sec = (1 - s) if side == 0 else s
            for q in range(1, hid):
                at = lax.rem(h + q, hid)
                c = remote(term_ref.at[rows, cols(sec, at)], hbuf.at[side, q, rows, :], (hs, hr),
                           (k * 2 + side) * hid + q, {"hid": at})
                c.start()
                first.append(c)
    across = []
    where = 0
    for k in range(MOST):
        rows = pl.ds(k * BLK, BLK)
        for side in range(2):
            sec = (1 - s) if side == 0 else s
            total = term_ref[rows, cols(sec, h)].astype(jnp.float32)
            for q in range(1, hid):
                first[where].wait_recv()
                where += 1
                total = total + hbuf[side, q, rows, :].astype(jnp.float32)
            if side == 0:
                ysend[rows, :] = total.astype(ysend.dtype)
                c = remote(ysend.at[rows, :], ybuf.at[rows, :], (ys, yr), k, {"sec": 1 - s})
                c.start()
                across.append(c)
            else:
                red[k] = total
    for k in range(MOST):
        rows = pl.ds(k * BLK, BLK)
        across[k].wait_recv()
        red[k] = red[k] + ybuf[rows, :].astype(jnp.float32)
    for b in range(spread.shape[0]):
        spread[b] = red[slot_ref[b]] * fac_ref[b * BLK:(b + 1) * BLK, :]

    def part(dest):
        return spread[dest * tl // BLK, pl.ds(pl.multiple_of(lax.rem(dest * tl, BLK), tl), tl), :]

    order = [k for k in range(1, n)] + [0]
    near = {}
    for k in order:
        j = lax.rem(i + k, n)
        psend[k] = part(j * 2 + 1 - par).astype(psend.dtype)
        c = remote(psend.at[k], pbuf.at[k], (xs, xr), k, {"exp": i * 2 + 1 - par})
        c.start()
        near[k] = c
    far = []
    for k in order:
        j = lax.rem(i + k, n)
        mine = part(j * 2 + par)
        near[k].wait_recv()
        mine = mine + pbuf[k].astype(jnp.float32)
        if k:
            qsend[k] = mine.astype(qsend.dtype)
            c = remote(qsend.at[k], qbuf.at[k], (zs, zr), k, {"exp": j * 2 + par})
            c.start()
            far.append(c)
        else:
            total = mine
    for k in range(1, n):
        far[k - 1].wait_recv()
        total = total + qbuf[k].astype(jnp.float32)
    out_ref[...] = total.astype(out_ref.dtype)
    for c in first + across + list(near.values()) + far:
        c.wait_send()


def per_device(tokens, norm_gain, route_weight, block_experts, w_gate, w_up, w_down):
    exp_devices = lax.axis_size("exp")
    hid = lax.axis_size("hid")
    n = exp_devices // 2
    group_size = exp_devices // EXPERTS
    my_expert = lax.axis_index("exp") // group_size
    tl, width = tokens.shape
    total_rows = tl * exp_devices
    num_blocks = total_rows // BLK
    slots = MOST * BLK
    model = w_gate.shape[1]
    hit = jnp.any(block_experts == my_expert, axis=1)
    ids = jnp.arange(num_blocks, dtype=jnp.int32)
    earlier = (ids[None, :] < ids[:, None]) & hit[None, :]
    slot_of_block = jnp.sum(earlier.astype(jnp.int32), axis=1)
    match = hit[None, :] & (slot_of_block[None, :] == jnp.arange(MOST, dtype=jnp.int32)[:, None])
    block_of_slot = jnp.sum(jnp.where(match, ids[None, :], 0), axis=1).astype(jnp.int32)
    safe_slot = jnp.where(hit, slot_of_block, 0).astype(jnp.int32)

    vmem = pl.BlockSpec(memory_space=pltpu.VMEM)
    smem = pl.BlockSpec(memory_space=pltpu.SMEM)
    dma = pltpu.SemaphoreType.DMA
    bf = jnp.bfloat16
    normed = pl.pallas_call(
        functools.partial(gather_kernel, n, hid),
        out_shape=jax.ShapeDtypeStruct((slots, model), bf),
        in_specs=[vmem, vmem, smem],
        out_specs=vmem,
        scratch_shapes=[
            pltpu.VMEM((num_blocks, BLK, width), bf),
            pltpu.VMEM((2 * hid, slots + EXTRA, width), bf),
            dma((n,)), dma((n,)), dma((n,)), dma((n,)), dma((MOST,)), dma((MOST,)),
            dma((MOST * hid,)), dma((MOST * hid,)), dma((MOST * hid,)), dma((MOST * hid,)),
        ],
        compiler_params=pltpu.CompilerParams(
            collective_id=0, has_side_effects=True, vmem_limit_bytes=32 * 2**20),
    )(tokens, norm_gain.reshape(1, width), block_of_slot)

    weights = lax.all_gather(route_weight, "exp", axis=0, tiled=True)
    chosen = jnp.repeat(block_experts == my_expert, BLK, axis=0)
    factor = jnp.sum(jnp.where(chosen, weights, 0.0), axis=1, keepdims=True)

    gate = jnp.dot(normed, w_gate[0], preferred_element_type=jnp.float32)
    up = jnp.dot(normed, w_up[0], preferred_element_type=jnp.float32)
    act = (jax.nn.silu(gate) * up).astype(bf)
    terms = jnp.dot(act, w_down[0], preferred_element_type=jnp.float32).astype(bf)

    return pl.pallas_call(
        functools.partial(reduce_kernel, n, hid),
        out_shape=jax.ShapeDtypeStruct((tl, width), bf),
        in_specs=[vmem, vmem, smem],
        out_specs=vmem,
        scratch_shapes=[
            pltpu.VMEM((2, hid, slots, width), bf),
            pltpu.VMEM((slots, width), bf),
            pltpu.VMEM((slots, width), bf),
            pltpu.VMEM((MOST, BLK, width), jnp.float32),
            pltpu.VMEM((num_blocks, BLK, width), jnp.float32),
            pltpu.VMEM((n, tl, width), bf),
            pltpu.VMEM((n, tl, width), bf),
            pltpu.VMEM((n, tl, width), bf),
            pltpu.VMEM((n, tl, width), bf),
            dma((2 * MOST * hid,)), dma((2 * MOST * hid,)), dma((MOST,)), dma((MOST,)),
            dma((n,)), dma((n,)), dma((n,)), dma((n,)),
        ],
        compiler_params=pltpu.CompilerParams(
            collective_id=1, has_side_effects=True, vmem_limit_bytes=40 * 2**20),
    )(terms, factor, safe_slot)


def solution(mesh):
    return jax.shard_map(
        per_device,
        mesh=mesh,
        in_specs=(
            P("exp", ("sec", "hid")),
            P(("sec", "hid")),
            P("exp", None),
            P(),
            P("sec", None, ("exp", "hid")),
            P("sec", None, ("exp", "hid")),
            P("sec", ("exp", "hid"), None),
        ),
        out_specs=P("exp", ("sec", "hid")),
        check_vma=False,
    )
```

time: 258 us -> 199 us (0.77)
  waiting for transfers between devices: 174 us -> 0 us
  Pallas kernels: 0 us -> 121 us
  blocking collectives: 5.16 us -> 23.4 us
  between operations: 13.2 us -> 0.05 us
  other arithmetic: 8.95 us -> 0.96 us
  starting transfers between devices: 5.6 us -> 0 us
    pallas_call x0 -> x2, Pallas kernels: none -> 121 us  [the longest x1 64 us: per_device(): pl.pallas_call(functools.partial(gather_kernel, n, hid), out_shape=jax.Sh...]
    all_gather x2 -> x0, waiting for transfers between devices: 80.9 us -> none  [the longest x1 53 us: per_device(): gathered = lax.all_gather(tokens, 'exp', axis=0, tiled=True)]
    all_to_all x1 -> x0, waiting for transfers between devices: 47.3 us -> none  [per_device(): lax.all_to_all(outgoing.astype(jnp.bfloat16), 'exp', split_axis=0, concat...]
    reduce_scatter x1 -> x0, waiting for transfers between devices: 44.7 us -> none  [per_device(): lax.psum_scatter(term_vals, ('sec', 'hid'), scatter_dimension=1, tiled=True)]
    all_gather x1, blocking collectives: 5.16 us -> 23.4 us  [per_device(): weights = lax.all_gather(route_weight, 'exp', axis=0, tiled=True)]
    unnamed x9 -> x10, local copies, waits for them, and re-layouts: 0.3 us -> 5.88 us
    all_to_all x1 -> x0, starting transfers between devices: 5.52 us -> none  [per_device(): lax.all_to_all(outgoing.astype(jnp.bfloat16), 'exp', split_axis=0, concat...]
    gather x3 -> x0, local copies, waits for them, and re-layouts: 4.75 us -> none  [the longest x1 2.2 us: per_device(): jnp.take(gathered.reshape(num_blocks, BLK, width), block_of_slot, axis=0)]
  transfers between devices with their start and end apart: 4 -> 0, of which waited for: 4 -> 0; matrix products, arithmetic and copies ran while one was open for 1% -> 0% of each run, Pallas kernels for 0% -> 0%
where the time goes in v1:
time: 199 us; the launch traced here: 197 us
  Pallas kernels  121 us (61%)
  matrix products  45.1 us (23%)
  blocking collectives  23.4 us (12%)
  local copies, waits for them, and re-layouts  6.79 us (3%)
    pallas_call x1, Pallas kernels, per_device(): pl.pallas_call(functools.partial(gather_kernel, n, hid), out_shape=jax.Sh...  64 us
    pallas_call x1, Pallas kernels, per_device(): pl.pallas_call(functools.partial(reduce_kernel, n, hid), out_shape=jax.Sh...  56.7 us
    dot_general x1, matrix products, per_device(): jnp.dot(act, w_down[0], preferred_element_type=jnp.float32).astype(bf)  31.3 us
    all_gather x1, blocking collectives, per_device(): weights = lax.all_gather(route_weight, 'exp', axis=0, tiled=True)  23.4 us
    dot_general x1, matrix products, per_device(): gate = jnp.dot(normed, w_gate[0], preferred_element_type=jnp.float32)  13.9 us
    unnamed x10, local copies, waits for them, and re-layouts  5.88 us

profile of v1, /device:TPU:0, one launch (start us, length us, event | category | flops | bytes accessed | tf_op | source)
XLA Modules:
  0.0 197.0 jit_solution(39781390326064498)
XLA Ops:
  0.0 0.7 fusion.18
  0.7 0.1 convert_reduce_fusion
  0.8 0.1 select_reduce_fusion.bos_ref
  0.9 0.7 reshape.8.gain_ref
  1.6 0.0 copy-start.2
  1.6 0.9 copy-done.2
  2.6 64.0 %shard_map.73 = bf16[512,4096]{1,0:T(8,128)(2,1)S(1)} custom-call(bf16[128,1024]{1,0:T(8,128)(2,1)S(1)} %copy-done.2, bf16[1,1024]{1,0:T(2,128)(2,1)S(1)} %reshape.8.gain_ref, s32[4]{0:T(128)S(1)} %select_reduce_fusion.bos_ref), custom_call_target="tpu_custom_call" | custom-call | tf_op jit(solution)/shard_map/pallas_call | solution.py:211
  66.6 0.0 copy-start.1
  66.6 2.0 copy-done.1
  68.5 13.9 %fusion.4 = f32[512,2048]{1,0:T(8,128)} fusion(bf16[512,4096]{1,0:T(8,128)(2,1)S(1)} %shard_map.73, bf16[1,4096,2048]{2,1,0:T(8,128)(2,1)} %param.11), kind=kOutput, calls=%fused_computation.4 | convolution fusion | flops 8589934592 | bytes 25165824 | tf_op jit(solution)/shard_map/dot_general | solution.py:230
  82.4 0.0 copy-start.3
  82.4 31.3 %fusion.6.term_ref = bf16[512,4096]{1,0:T(8,128)(2,1)} fusion(bf16[1,2048,4096]{2,1,0:T(8,128)(2,1)} %param.13, f32[512,2048]{1,0:T(8,128)} %fusion.4, bf16[512,4096]{1,0:T(8,128)(2,1)} %copy-done.1, bf16[1,4096,2048]{2,1,0:T(8,128)(2,1)} %param.12), kind=kOutput, calls=%fused_computation.6 | convolution fusion | flops 17188257792 | bytes 46137344 | tf_op jit(solution)/shard_map/dot_general | solution.py:233
  113.7 0.1 broadcast_bitcast_fusion
  113.7 0.0 copy-done.3
  113.7 23.4 %all_gather.3 = f32[1024,2]{0,1:T(2,128)S(1)} all-gather(f32[128,2]{0,1:T(2,128)S(1)} %copy-done.3), channel_id=1, replica_groups=mesh['sec'=2,'exp'=8,'hid'=2] {'exp'}, dimensions={0}, use_global_device_ids=true | all-gather | bytes 9216 | tf_op jit(solution)/shard_map/all_gather | solution.py:226
  137.2 0.2 copy.9.fac_ref
  137.4 0.0 copy-start
  137.4 2.2 %copy-done = bf16[512,4096]{1,0:T(8,128)(2,1)S(1)} copy-done((bf16[512,4096]{1,0:T(8,128)(2,1)S(1)}, bf16[512,4096]{1,0:T(8,128)(2,1)}, u32[]{:S(2)}) %copy-start) | copy-done | bytes 4194328
  139.6 56.7 %shard_map.74 = bf16[128,1024]{1,0:T(8,128)(2,1)S(1)} custom-call(bf16[512,4096]{1,0:T(8,128)(2,1)S(1)} %copy-done, f32[1024,1]{1,0:T(8,128)S(1)} %copy.9.fac_ref, s32[8]{0:T(128)S(1)} %broadcast_select_fusion.slot_ref), custom_call_target="tpu_custom_call" | custom-call | tf_op jit(solution)/shard_map/pallas_call | solution.py:235
  196.3 0.7 copy.15
  (2 shorter events, 0.0 us)
Async XLA Ops:
  1.6 0.9 copy-start.2
  66.6 2.0 %copy-start.1 = (bf16[512,4096]{1,0:T(8,128)(2,1)}, bf16[512,4096]{1,0:T(8,128)(2,1)S(1)}, u32[]{:S(2)}) copy-start(bf16[512,4096]{1,0:T(8,128)(2,1)S(1)} %shard_map.73) | copy-start | bytes 12582916
  82.4 31.3 %copy-start.3 = (f32[128,2]{0,1:T(2,128)S(1)}, f32[128,2]{0,1:T(2,128)}, u32[]{:S(2)}) copy-start(f32[128,2]{0,1:T(2,128)} %param.9) | copy-start | bytes 3076
  137.4 2.2 %copy-start = (bf16[512,4096]{1,0:T(8,128)(2,1)S(1)}, bf16[512,4096]{1,0:T(8,128)(2,1)}, u32[]{:S(2)}) copy-start(bf16[512,4096]{1,0:T(8,128)(2,1)} %fusion.6.term_ref) | copy-start | bytes 12582916

commit v2 on v1

--- a/solution.py
+++ b/solution.py
@@ -36,60 +36,90 @@
     )
 
 
-def gather_kernel(n, hid, tok_ref, gain_ref, bos_ref, out_ref, gathered, full,
-                  zs, zr, xs, xr, ys, yr, hs, hr, gs, gr):
+def gather_kernel(n, hid, chunks, tok_ref, gain_ref, rw_ref, bos_ref, out_ref, rw_out, full, gw, *rest):
+    gathered = rest[:chunks]
+    zs, zr, xs, xr, ys, yr, hs, hr, gs, gr, ws, wr, vs, vr = rest[chunks:]
     e, i, par, s, h = greet(n, hid)
-    tl, width = tok_ref.shape
+    tl = tok_ref.shape[0]
+    half = full.shape[2]
     slots = MOST * BLK
-
-    def rows_of(index):
-        return gathered.at[index * tl // BLK, pl.ds(pl.multiple_of(lax.rem(index * tl, BLK), tl), tl), :]
-
-    mine = rows_of(e)
-    mine[...] = tok_ref[...]
+    groups = full.shape[0]
     pair = {"exp": i * 2 + 1 - par}
-    far = []
-    for k in range(1, n):
-        c = remote(mine, mine, (zs, zr), k, {"exp": lax.rem(i + k, n) * 2 + par})
-        c.start()
-        far.append(c)
-    near = [remote(mine, mine, (xs, xr), 0, pair)]
-    near[0].start()
-    for k in range(1, n):
-        far[k - 1].wait_recv()
-        got = rows_of(lax.rem(i - k + n, n) * 2 + par)
-        c = remote(got, got, (xs, xr), k, pair)
-        c.start()
-        near.append(c)
-    for c in near:
-        c.wait_recv()
-
     me = s * hid + h
     over = (1 - s) * hid + h
-    full[me, slots:, :] = jnp.broadcast_to(gain_ref[...], (EXTRA, width))
     parts = [pl.ds(k * BLK, BLK) for k in range(MOST)]
     parts[-1] = pl.ds((MOST - 1) * BLK, BLK + EXTRA)
-    side, own, passed = [], [], []
-    for k in range(MOST):
-        full[me, k * BLK:(k + 1) * BLK, :] = gathered[bos_ref[k]]
-        ref = full.at[me, parts[k], :]
-        c = remote(ref, ref, (ys, yr), k, {"sec": 1 - s})
-        c.start()
-        side.append(c)
-        for q in range(1, hid):
-            c = remote(ref, ref, (hs, hr), k * hid + q, {"hid": lax.rem(h + q, hid)})
-            c.start()
-            own.append(c)
-    for k in range(MOST):
-        side[k].wait_recv()
-        ref = full.at[over, parts[k], :]
-        for q in range(1, hid):
-            c = remote(ref, ref, (gs, gr), k * hid + q, {"hid": lax.rem(h + q, hid)})
-            c.start()
-            passed.append(c)
-    for c in own + passed:
-        c.wait_recv()
-    groups = 2 * hid
+    far, near, side, passed = {}, {}, {}, []
+
+    def rows_of(c, index):
+        return gathered[c].at[index * tl // BLK, pl.ds(pl.multiple_of(lax.rem(index * tl, BLK), tl), tl), :]
+
+    def start(c):
+        mine = rows_of(c, e)
+        mine[...] = tok_ref[:, c * half:(c + 1) * half]
+        for k in range(1, n):
+            far[c, k] = remote(mine, mine, (zs, zr), c * n + k, {"exp": lax.rem(i + k, n) * 2 + par})
+            far[c, k].start()
+        near[c, 0] = remote(mine, mine, (xs, xr), c * n, pair)
+        near[c, 0].start()
+
+    def forward(c):
+        for k in range(1, n):
+            far[c, k].wait_recv()
+            got = rows_of(c, lax.rem(i - k + n, n) * 2 + par)
+            near[c, k] = remote(got, got, (xs, xr), c * n + k, pair)
+            near[c, k].start()
+
+    def pick(c):
+        for k in range(n):
+            near[c, k].wait_recv()
+        spot = me * chunks + c
+        full[spot, slots:, :] = jnp.broadcast_to(gain_ref[:, c * half:(c + 1) * half], (EXTRA, half))
+        for k in range(MOST):
+            full[spot, k * BLK:(k + 1) * BLK, :] = gathered[c][bos_ref[k]]
+            ref = full.at[spot, parts[k], :]
+            at = c * MOST + k
+            side[c, k] = remote(ref, ref, (ys, yr), at, {"sec": 1 - s})
+            side[c, k].start()
+            for q in range(1, hid):
+                copy = remote(ref, ref, (hs, hr), at * hid + q, {"hid": lax.rem(h + q, hid)})
+                copy.start()
+                passed.append(copy)
+
+    def share(c):
+        for k in range(MOST):
+            side[c, k].wait_recv()
+            ref = full.at[over * chunks + c, parts[k], :]
+            for q in range(1, hid):
+                copy = remote(ref, ref, (gs, gr), (c * MOST + k) * hid + q, {"hid": lax.rem(h + q, hid)})
+                copy.start()
+                passed.append(copy)
+
+    gw[e] = rw_ref[...]
+    wfar, wnear = [], [remote(gw.at[e], gw.at[e], (vs, vr), 0, pair)]
+    start(0)
+    for k in range(1, n):
+        copy = remote(gw.at[e], gw.at[e], (ws, wr), k, {"exp": lax.rem(i + k, n) * 2 + par})
+        copy.start()
+        wfar.append(copy)
+    wnear[0].start()
+    for t in range(chunks + 2):
+        if 0 <= t - 2:
+            share(t - 2)
+        if 0 <= t - 1 < chunks:
+            pick(t - 1)
+        if t < chunks:
+            forward(t)
+        if t + 1 < chunks:
+            start(t + 1)
+    for k in range(1, n):
+        wfar[k - 1].wait_recv()
+        got = gw.at[lax.rem(i - k + n, n) * 2 + par]
+        copy = remote(got, got, (vs, vr), k, pair)
+        copy.start()
+        wnear.append(copy)
+    for copy in passed:
+        copy.wait_recv()
 
     def norm(step, carry):
         rows = pl.ds(pl.multiple_of(step * 32, 32), 32)
@@ -97,16 +127,35 @@
         for j in range(groups):
             v = full[j, rows, :].astype(jnp.float32)
             total = total + jnp.sum(v * v, axis=1, keepdims=True)
-        rms = jnp.sqrt(total / (groups * width) + 1e-05)
+        rms = jnp.sqrt(total / (groups * half) + 1e-05)
         for j in range(groups):
             v = full[j, rows, :].astype(jnp.float32)
             gain = full[j, slots:slots + EXTRA, :].astype(jnp.float32)[0:1, :]
-            out_ref[rows, j * width:(j + 1) * width] = (v * gain / rms).astype(out_ref.dtype)
+            out_ref[rows, j * half:(j + 1) * half] = (v * gain / rms).astype(out_ref.dtype)
         return carry
 
     lax.fori_loop(0, slots // 32, norm, 0)
-    for c in far + near + side + own + passed:
-        c.wait_send()
+    for copy in wnear:
+        copy.wait_recv()
+    rw_out[...] = gw[...]
+    for copy in list(far.values()) + list(near.values()) + list(side.values()) + passed + wfar + wnear:
+        copy.wait_send()
+
+
+def ffn_kernel(first, tile, x_ref, gate_ref, up_ref, down_ref, out_ref, act):
+    j = pl.program_id(0)
+
+    @pl.when(j < first)
+    def _():
+        x = x_ref[...]
+        gate = jnp.dot(x, gate_ref[0], preferred_element_type=jnp.float32)
+        up = jnp.dot(x, up_ref[0], preferred_element_type=jnp.float32)
+        vals = gate / (1.0 + jnp.exp(-gate)) * up
+        act[:, pl.ds(pl.multiple_of(j * tile, tile), tile)] = vals.astype(act.dtype)
+
+    @pl.when(j >= first)
+    def _():
+        out_ref[...] = jnp.dot(act[...], down_ref[0], preferred_element_type=jnp.float32).astype(out_ref.dtype)
 
 
 def reduce_kernel(n, hid, term_ref, fac_ref, slot_ref, out_ref, hbuf, ysend, ybuf, red, spread,
@@ -208,29 +257,56 @@
     smem = pl.BlockSpec(memory_space=pltpu.SMEM)
     dma = pltpu.SemaphoreType.DMA
     bf = jnp.bfloat16
-    normed = pl.pallas_call(
-        functools.partial(gather_kernel, n, hid),
-        out_shape=jax.ShapeDtypeStruct((slots, model), bf),
-        in_specs=[vmem, vmem, smem],
-        out_specs=vmem,
+    chunks = 2 if width % 256 == 0 else 1
+    half = width // chunks
+    lanes = max(BLK, tl)
+    packed = jnp.zeros((8, lanes), jnp.float32).at[:route_weight.shape[1], :tl].set(route_weight.T)
+    normed, weights = pl.pallas_call(
+        functools.partial(gather_kernel, n, hid, chunks),
+        out_shape=(
+            jax.ShapeDtypeStruct((slots, model), bf),
+            jax.ShapeDtypeStruct((exp_devices, 8, lanes), jnp.float32),
+        ),
+        in_specs=[vmem, vmem, vmem, smem],
+        out_specs=(vmem, vmem),
         scratch_shapes=[
-            pltpu.VMEM((num_blocks, BLK, width), bf),
-            pltpu.VMEM((2 * hid, slots + EXTRA, width), bf),
-            dma((n,)), dma((n,)), dma((n,)), dma((n,)), dma((MOST,)), dma((MOST,)),
-            dma((MOST * hid,)), dma((MOST * hid,)), dma((MOST * hid,)), dma((MOST * hid,)),
+            pltpu.VMEM((2 * hid * chunks, slots + EXTRA, half), bf),
+            pltpu.VMEM((exp_devices, 8, lanes), jnp.float32),
+            *[pltpu.VMEM((num_blocks, BLK, half), bf)] * chunks,
+            *[dma((chunks * n,))] * 4,
+            *[dma((chunks * MOST,))] * 2,
+            *[dma((chunks * MOST * hid,))] * 4,
+            *[dma((n,))] * 4,
         ],
         compiler_params=pltpu.CompilerParams(
             collective_id=0, has_side_effects=True, vmem_limit_bytes=32 * 2**20),
-    )(tokens, norm_gain.reshape(1, width), block_of_slot)
-
-    weights = lax.all_gather(route_weight, "exp", axis=0, tiled=True)
+    )(tokens, norm_gain.reshape(1, width), packed, block_of_slot)
+
+    weights = weights[:, :route_weight.shape[1], :tl].transpose(0, 2, 1).reshape(total_rows, -1)
     chosen = jnp.repeat(block_experts == my_expert, BLK, axis=0)
     factor = jnp.sum(jnp.where(chosen, weights, 0.0), axis=1, keepdims=True)
 
-    gate = jnp.dot(normed, w_gate[0], preferred_element_type=jnp.float32)
-    up = jnp.dot(normed, w_up[0], preferred_element_type=jnp.float32)
-    act = (jax.nn.silu(gate) * up).astype(bf)
-    terms = jnp.dot(act, w_down[0], preferred_element_type=jnp.float32).astype(bf)
+    units = w_gate.shape[2]
+    tile = min(256, units)
+    first = units // tile
+    out_tile = min(512, model)
+    flops = 6 * slots * model * units
+    terms = pl.pallas_call(
+        functools.partial(ffn_kernel, first, tile),
+        grid=(first + model // out_tile,),
+        out_shape=jax.ShapeDtypeStruct((slots, model), bf),
+        in_specs=[
+            pl.BlockSpec((slots, model), lambda j: (0, 0)),
+            pl.BlockSpec((1, model, tile), lambda j: (0, 0, jnp.minimum(j, first - 1))),
+            pl.BlockSpec((1, model, tile), lambda j: (0, 0, jnp.minimum(j, first - 1))),
+            pl.BlockSpec((1, units, out_tile), lambda j: (0, 0, jnp.maximum(j - first, 0))),
+        ],
+        out_specs=pl.BlockSpec((slots, out_tile), lambda j: (0, jnp.maximum(j - first, 0))),
+        scratch_shapes=[pltpu.VMEM((slots, units), bf)],
+        compiler_params=pltpu.CompilerParams(vmem_limit_bytes=40 * 2**20),
+        cost_estimate=pl.CostEstimate(
+            flops=flops, bytes_accessed=6 * model * units, transcendentals=slots * units),
+    )(normed, w_gate, w_up, w_down)
 
     return pl.pallas_call(
         functools.partial(reduce_kernel, n, hid),

time: 199 us -> 155 us (0.78)
  matrix products: 45.1 us -> 0 us
  Pallas kernels: 121 us -> 146 us
  blocking collectives: 23.4 us -> 0 us
    dot_general x2 -> x0, matrix products: 45.1 us -> none  [the longest x1 31.3 us: per_device(): jnp.dot(act, w_down[0], preferred_element_type=jnp.float32).astype(bf)]
    all_gather x1 -> x0, blocking collectives: 23.4 us -> none  [per_device(): weights = lax.all_gather(route_weight, 'exp', axis=0, tiled=True)]
    pallas_call x1 -> x2, Pallas kernels: 64 us -> 84.1 us  [the longest x1 50.4 us: per_device(): pl.pallas_call(functools.partial(gather_kernel, n, hid, chunks), out_shap...]
    pallas_call x1, Pallas kernels: 56.7 us -> 61.6 us  [per_device(): pl.pallas_call(functools.partial(reduce_kernel, n, hid), out_shape=jax.Sh...]
    unnamed x10 -> x7, local copies, waits for them, and re-layouts: 5.88 us -> 5.76 us
where the time goes in v2:
time: 155 us; the launch traced here: 154 us
  Pallas kernels  146 us (94%)
  local copies, waits for them, and re-layouts  7.45 us (5%)
    pallas_call x1, Pallas kernels, per_device(): pl.pallas_call(functools.partial(reduce_kernel, n, hid), out_shape=jax.Sh...  61.6 us
    pallas_call x1, Pallas kernels, per_device(): pl.pallas_call(functools.partial(gather_kernel, n, hid, chunks), out_shap...  50.4 us
    pallas_call x1, Pallas kernels, per_device(): pl.pallas_call(functools.partial(ffn_kernel, first, tile), grid=(first +...  33.7 us
    unnamed x7, local copies, waits for them, and re-layouts  5.76 us

profile of v2, /device:TPU:0, one launch (start us, length us, event | category | flops | bytes accessed | tf_op | source)
XLA Modules:
  0.0 154.2 jit_solution(10984940879245407949)
XLA Ops:
  0.0 0.7 fusion.2
  0.7 0.1 convert_reduce_fusion
  0.8 0.1 select_reduce_fusion.1.bos_ref
  0.9 0.1 copy.11
  1.0 0.7 reshape.35.gain_ref
  1.7 0.7 scatter.4.rw_ref
  2.4 0.0 copy-start.2
  2.4 0.9 copy-done.2
  3.4 50.4 %shard_map.73 = (bf16[512,4096]{1,0:T(8,128)(2,1)S(1)}, f32[8,8,128]{2,1,0:T(8,128)S(1)}) custom-call(bf16[128,1024]{1,0:T(8,128)(2,1)S(1)} %copy-done.2, bf16[1,1024]{1,0:T(2,128)(2,1)S(1)} %reshape.35.gain_ref, f32[8,128]{1,0:T(8,128)S(1)} %scatter.4.rw_ref, s32[4]{0:T(128)S(1)} %select_reduce_fusion.1.bos_ref), custom_call_target="tpu_custom_call" | custom-call | tf_op jit(solution)/shard_map/pallas_call | solution.py:264
  53.8 33.7 %shard_map.74.term_ref = bf16[512,4096]{1,0:T(8,128)(2,1)S(1)} custom-call(bf16[512,4096]{1,0:T(8,128)(2,1)S(1)} %get-tuple-element.19.x_ref, bf16[1,4096,2048]{2,1,0:T(8,128)(2,1)} %gate_ref.1, bf16[1,4096,2048]{2,1,0:T(8,128)(2,1)} %up_ref.1, bf16[1,2048,4096]{2,1,0:T(8,128)(2,1)} %down_ref.1), custom_call_target="tpu_custom_call" | custom-call | flops 25769803776 | bytes 50331648 | tf_op jit(solution)/shard_map/pallas_call | solution.py:294
  87.4 0.0 copy-start
  87.4 1.9 %copy-done = bf16[512,4096]{1,0:T(8,128)(2,1)} copy-done((bf16[512,4096]{1,0:T(8,128)(2,1)}, bf16[512,4096]{1,0:T(8,128)(2,1)S(1)}, u32[]{:S(2)}) %copy-start) | copy-done | bytes 4194328
  89.4 0.1 select_reduce_fusion
  89.4 0.2 copy.12.fac_ref
  89.7 0.0 copy-start.1
  89.7 2.2 %copy-done.1 = bf16[512,4096]{1,0:T(8,128)(2,1)S(1)} copy-done((bf16[512,4096]{1,0:T(8,128)(2,1)S(1)}, bf16[512,4096]{1,0:T(8,128)(2,1)}, u32[]{:S(2)}) %copy-start.1) | copy-done | bytes 4194328
  91.9 61.6 %shard_map.75 = bf16[128,1024]{1,0:T(8,128)(2,1)S(1)} custom-call(bf16[512,4096]{1,0:T(8,128)(2,1)S(1)} %copy-done.1, f32[1024,1]{1,0:T(8,128)S(1)} %copy.12.fac_ref, s32[8]{0:T(128)S(1)} %broadcast_select_fusion.slot_ref), custom_call_target="tpu_custom_call" | custom-call | tf_op jit(solution)/shard_map/pallas_call | solution.py:311
  153.5 0.7 copy.14
  (1 shorter events, 0.0 us)
Async XLA Ops:
  2.4 0.9 copy-start.2
  87.4 1.9 %copy-start = (bf16[512,4096]{1,0:T(8,128)(2,1)}, bf16[512,4096]{1,0:T(8,128)(2,1)S(1)}, u32[]{:S(2)}) copy-start(bf16[512,4096]{1,0:T(8,128)(2,1)S(1)} %shard_map.74.term_ref) | copy-start | bytes 12582916
  89.7 2.2 %copy-start.1 = (bf16[512,4096]{1,0:T(8,128)(2,1)S(1)}, bf16[512,4096]{1,0:T(8,128)(2,1)}, u32[]{:S(2)}) copy-start(bf16[512,4096]{1,0:T(8,128)(2,1)} %copy-done) | copy-start | bytes 12582916

commit v3 on v2

--- a/solution.py
+++ b/solution.py
@@ -158,80 +158,94 @@
         out_ref[...] = jnp.dot(act[...], down_ref[0], preferred_element_type=jnp.float32).astype(out_ref.dtype)
 
 
-def reduce_kernel(n, hid, term_ref, fac_ref, slot_ref, out_ref, hbuf, ysend, ybuf, red, spread,
-                  psend, pbuf, qsend, qbuf, hs, hr, ys, yr, xs, xr, zs, zr):
+def reduce_kernel(n, hid, chunks, term_ref, fac_ref, slot_ref, out_ref, hbuf, ysend, ybuf, spread,
+                  psend, pbuf, qsend, qbuf, *rest):
+    red = rest[:chunks]
+    hs, hr, ys, yr, xs, xr, zs, zr = rest[chunks:]
     e, i, par, s, h = greet(n, hid)
     tl, width = out_ref.shape
-
-    def cols(sec, at):
-        return pl.ds(pl.multiple_of((sec * hid + at) * width, width), width)
-
-    first = []
-    for k in range(MOST):
-        rows = pl.ds(k * BLK, BLK)
+    half = width // chunks
+    order = [k for k in range(1, n)] + [0]
+    pair = {"exp": i * 2 + 1 - par}
+    first, across, near, far, own = {}, {}, {}, {}, {}
+
+    def cols(side, at, c):
+        sec = (1 - s) if side == 0 else s
+        return pl.ds(pl.multiple_of((sec * hid + at) * width + c * half, half), half)
+
+    def swap(c):
         for side in range(2):
-            sec = (1 - s) if side == 0 else s
             for q in range(1, hid):
                 at = lax.rem(h + q, hid)
-                c = remote(term_ref.at[rows, cols(sec, at)], hbuf.at[side, q, rows, :], (hs, hr),
-                           (k * 2 + side) * hid + q, {"hid": at})
-                c.start()
-                first.append(c)
-    across = []
-    where = 0
-    for k in range(MOST):
-        rows = pl.ds(k * BLK, BLK)
+                first[c, side, q] = remote(
+                    term_ref.at[:, cols(side, at, c)], hbuf.at[c * 2 + side, q], (hs, hr),
+                    (c * 2 + side) * hid + q, {"hid": at})
+                first[c, side, q].start()
+
+    def cross(c):
         for side in range(2):
-            sec = (1 - s) if side == 0 else s
-            total = term_ref[rows, cols(sec, h)].astype(jnp.float32)
             for q in range(1, hid):
-                first[where].wait_recv()
-                where += 1
-                total = total + hbuf[side, q, rows, :].astype(jnp.float32)
+                first[c, side, q].wait_recv()
+            for k in range(MOST):
+                rows = pl.ds(k * BLK, BLK)
+                total = term_ref[rows, cols(side, h, c)].astype(jnp.float32)
+                for q in range(1, hid):
+                    total = total + hbuf[c * 2 + side, q, rows, :].astype(jnp.float32)
+                if side == 0:
+                    ysend[c, rows, :] = total.astype(ysend.dtype)
+                else:
+                    red[c][k] = total
             if side == 0:
-                ysend[rows, :] = total.astype(ysend.dtype)
-                c = remote(ysend.at[rows, :], ybuf.at[rows, :], (ys, yr), k, {"sec": 1 - s})
-                c.start()
-                across.append(c)
+                across[c] = remote(ysend.at[c], ybuf.at[c], (ys, yr), c, {"sec": 1 - s})
+                across[c].start()
+
+    def part(c, dest):
+        return spread[c, dest * tl // BLK, pl.ds(pl.multiple_of(lax.rem(dest * tl, BLK), tl), tl), :]
+
+    def weigh(c):
+        across[c].wait_recv()
+        for k in range(MOST):
+            red[c][k] = red[c][k] + ybuf[c, k * BLK:(k + 1) * BLK, :].astype(jnp.float32)
+        for b in range(spread.shape[1]):
+            spread[c, b] = red[c][slot_ref[b]] * fac_ref[b * BLK:(b + 1) * BLK, :]
+        for k in order:
+            at = c * n + k
+            psend[at] = part(c, lax.rem(i + k, n) * 2 + 1 - par).astype(psend.dtype)
+            near[c, k] = remote(psend.at[at], pbuf.at[at], (xs, xr), at, pair)
+            near[c, k].start()
+
+    def deliver(c):
+        for k in order:
+            at = c * n + k
+            dest = lax.rem(i + k, n) * 2 + par
+            near[c, k].wait_recv()
+            mine = part(c, dest) + pbuf[at].astype(jnp.float32)
+            if k:
+                qsend[at] = mine.astype(qsend.dtype)
+                far[c, k] = remote(qsend.at[at], qbuf.at[at], (zs, zr), at, {"exp": dest})
+                far[c, k].start()
             else:
-                red[k] = total
-    for k in range(MOST):
-        rows = pl.ds(k * BLK, BLK)
-        across[k].wait_recv()
-        red[k] = red[k] + ybuf[rows, :].astype(jnp.float32)
-    for b in range(spread.shape[0]):
-        spread[b] = red[slot_ref[b]] * fac_ref[b * BLK:(b + 1) * BLK, :]
-
-    def part(dest):
-        return spread[dest * tl // BLK, pl.ds(pl.multiple_of(lax.rem(dest * tl, BLK), tl), tl), :]
-
-    order = [k for k in range(1, n)] + [0]
-    near = {}
-    for k in order:
-        j = lax.rem(i + k, n)
-        psend[k] = part(j * 2 + 1 - par).astype(psend.dtype)
-        c = remote(psend.at[k], pbuf.at[k], (xs, xr), k, {"exp": i * 2 + 1 - par})
-        c.start()
-        near[k] = c
-    far = []
-    for k in order:
-        j = lax.rem(i + k, n)
-        mine = part(j * 2 + par)
-        near[k].wait_recv()
-        mine = mine + pbuf[k].astype(jnp.float32)
-        if k:
-            qsend[k] = mine.astype(qsend.dtype)
-            c = remote(qsend.at[k], qbuf.at[k], (zs, zr), k, {"exp": j * 2 + par})
-            c.start()
-            far.append(c)
-        else:
-            total = mine
-    for k in range(1, n):
-        far[k - 1].wait_recv()
-        total = total + qbuf[k].astype(jnp.float32)
-    out_ref[...] = total.astype(out_ref.dtype)
-    for c in first + across + list(near.values()) + far:
-        c.wait_send()
+                own[c] = mine
+
+    for c in range(chunks):
+        swap(c)
+    cross(0)
+    for t in range(chunks + 1):
+        if t + 1 < chunks:
+            cross(t + 1)
+        if t < chunks:
+            weigh(t)
+        if t >= 1:
+            deliver(t - 1)
+    for c in range(chunks):
+        total = own[c]
+        for k in range(1, n):
+            far[c, k].wait_recv()
+            total = total + qbuf[c * n + k].astype(jnp.float32)
+        out_ref[:, c * half:(c + 1) * half] = total.astype(out_ref.dtype)
+    for group in (first, across, near, far):
+        for copy in group.values():
+            copy.wait_send()
 
 
 def per_device(tokens, norm_gain, route_weight, block_experts, w_gate, w_up, w_down):
@@ -257,7 +271,7 @@
     smem = pl.BlockSpec(memory_space=pltpu.SMEM)
     dma = pltpu.SemaphoreType.DMA
     bf = jnp.bfloat16
-    chunks = 2 if width % 256 == 0 else 1
+    chunks = next(c for c in (4, 2, 1) if width % (c * BLK) == 0)
     half = width // chunks
     lanes = max(BLK, tl)
     packed = jnp.zeros((8, lanes), jnp.float32).at[:route_weight.shape[1], :tl].set(route_weight.T)
@@ -309,22 +323,19 @@
     )(normed, w_gate, w_up, w_down)
 
     return pl.pallas_call(
-        functools.partial(reduce_kernel, n, hid),
+        functools.partial(reduce_kernel, n, hid, chunks),
         out_shape=jax.ShapeDtypeStruct((tl, width), bf),
         in_specs=[vmem, vmem, smem],
         out_specs=vmem,
         scratch_shapes=[
-            pltpu.VMEM((2, hid, slots, width), bf),
-            pltpu.VMEM((slots, width), bf),
-            pltpu.VMEM((slots, width), bf),
-            pltpu.VMEM((MOST, BLK, width), jnp.float32),
-            pltpu.VMEM((num_blocks, BLK, width), jnp.float32),
-            pltpu.VMEM((n, tl, width), bf),
-            pltpu.VMEM((n, tl, width), bf),
-            pltpu.VMEM((n, tl, width), bf),
-            pltpu.VMEM((n, tl, width), bf),
-            dma((2 * MOST * hid,)), dma((2 * MOST * hid,)), dma((MOST,)), dma((MOST,)),
-            dma((n,)), dma((n,)), dma((n,)), dma((n,)),
+            pltpu.VMEM((2 * chunks, hid, slots, half), bf),
+            *[pltpu.VMEM((chunks, slots, half), bf)] * 2,
+            pltpu.VMEM((chunks, num_blocks, BLK, half), jnp.float32),
+            *[pltpu.VMEM((chunks * n, tl, half), bf)] * 4,
+            *[pltpu.VMEM((MOST, BLK, half), jnp.float32)] * chunks,
+            *[dma((2 * chunks * hid,))] * 2,
+            *[dma((chunks,))] * 2,
+            *[dma((chunks * n,))] * 4,
         ],
         compiler_params=pltpu.CompilerParams(
             collective_id=1, has_side_effects=True, vmem_limit_bytes=40 * 2**20),

time: 155 us -> 135 us (0.87)
  Pallas kernels: 146 us -> 126 us
    pallas_call x1, Pallas kernels: 61.6 us -> 41.9 us  [per_device(): pl.pallas_call(functools.partial(reduce_kernel, n, hid, chunks), out_shap...]
where the time goes in v3:
time: 135 us; the launch traced here: 134 us
  Pallas kernels  126 us (93%)
  local copies, waits for them, and re-layouts  7.45 us (6%)
    pallas_call x1, Pallas kernels, per_device(): pl.pallas_call(functools.partial(gather_kernel, n, hid, chunks), out_shap...  50 us
    pallas_call x1, Pallas kernels, per_device(): pl.pallas_call(functools.partial(reduce_kernel, n, hid, chunks), out_shap...  41.9 us
    pallas_call x1, Pallas kernels, per_device(): pl.pallas_call(functools.partial(ffn_kernel, first, tile), grid=(first +...  33.7 us
    unnamed x7, local copies, waits for them, and re-layouts  5.76 us

profile of v3, /device:TPU:0, one launch (start us, length us, event | category | flops | bytes accessed | tf_op | source)
XLA Modules:
  0.0 134.1 jit_solution(10445130685019223194)
XLA Ops:
  0.0 0.7 fusion.2
  0.7 0.1 convert_reduce_fusion
  0.8 0.1 select_reduce_fusion.1.bos_ref
  0.9 0.1 copy.11
  1.0 0.7 reshape.35.gain_ref
  1.7 0.7 scatter.4.rw_ref
  2.4 0.0 copy-start.2
  2.4 0.9 copy-done.2
  3.4 50.0 %shard_map.73 = (bf16[512,4096]{1,0:T(8,128)(2,1)S(1)}, f32[8,8,128]{2,1,0:T(8,128)S(1)}) custom-call(bf16[128,1024]{1,0:T(8,128)(2,1)S(1)} %copy-done.2, bf16[1,1024]{1,0:T(2,128)(2,1)S(1)} %reshape.35.gain_ref, f32[8,128]{1,0:T(8,128)S(1)} %scatter.4.rw_ref, s32[4]{0:T(128)S(1)} %select_reduce_fusion.1.bos_ref), custom_call_target="tpu_custom_call" | custom-call | tf_op jit(solution)/shard_map/pallas_call | solution.py:278
  53.4 33.7 %shard_map.74.term_ref = bf16[512,4096]{1,0:T(8,128)(2,1)S(1)} custom-call(bf16[512,4096]{1,0:T(8,128)(2,1)S(1)} %get-tuple-element.19.x_ref, bf16[1,4096,2048]{2,1,0:T(8,128)(2,1)} %gate_ref.1, bf16[1,4096,2048]{2,1,0:T(8,128)(2,1)} %up_ref.1, bf16[1,2048,4096]{2,1,0:T(8,128)(2,1)} %down_ref.1), custom_call_target="tpu_custom_call" | custom-call | flops 25769803776 | bytes 50331648 | tf_op jit(solution)/shard_map/pallas_call | solution.py:308
  87.1 0.0 copy-start
  87.1 1.9 %copy-done = bf16[512,4096]{1,0:T(8,128)(2,1)} copy-done((bf16[512,4096]{1,0:T(8,128)(2,1)}, bf16[512,4096]{1,0:T(8,128)(2,1)S(1)}, u32[]{:S(2)}) %copy-start) | copy-done | bytes 4194328
  89.0 0.1 select_reduce_fusion
  89.1 0.2 copy.12.fac_ref
  89.3 0.0 copy-start.1
  89.3 2.2 %copy-done.1 = bf16[512,4096]{1,0:T(8,128)(2,1)S(1)} copy-done((bf16[512,4096]{1,0:T(8,128)(2,1)S(1)}, bf16[512,4096]{1,0:T(8,128)(2,1)}, u32[]{:S(2)}) %copy-start.1) | copy-done | bytes 4194328
  91.5 41.9 %shard_map.75 = bf16[128,1024]{1,0:T(8,128)(2,1)S(1)} custom-call(bf16[512,4096]{1,0:T(8,128)(2,1)S(1)} %copy-done.1, f32[1024,1]{1,0:T(8,128)S(1)} %copy.12.fac_ref, s32[8]{0:T(128)S(1)} %broadcast_select_fusion.slot_ref), custom_call_target="tpu_custom_call" | custom-call | tf_op jit(solution)/shard_map/pallas_call | solution.py:325
  133.4 0.7 copy.14
  (1 shorter events, 0.0 us)
Async XLA Ops:
  2.4 0.9 copy-start.2
  87.1 1.9 %copy-start = (bf16[512,4096]{1,0:T(8,128)(2,1)}, bf16[512,4096]{1,0:T(8,128)(2,1)S(1)}, u32[]{:S(2)}) copy-start(bf16[512,4096]{1,0:T(8,128)(2,1)S(1)} %shard_map.74.term_ref) | copy-start | bytes 12582916
  89.3 2.2 %copy-start.1 = (bf16[512,4096]{1,0:T(8,128)(2,1)S(1)}, bf16[512,4096]{1,0:T(8,128)(2,1)}, u32[]{:S(2)}) copy-start(bf16[512,4096]{1,0:T(8,128)(2,1)} %copy-done) | copy-start | bytes 12582916
